TPU v7x, 256 devices: a whole 4x4x8 slice. The times are simulated.
256 devices in a mesh: dp: 32 (over y, z), tensor: 8 (over x, core).
Axes of the slice: x: 4, y: 4, z: 8, core: 2. Of those that a mesh axis runs over, the one named last changes fastest.
Arguments:
- context: bfloat16 [16384, 2048], P('dp', 'tensor'), may hold values from -6 to 6
- cotangent: bfloat16 [16384, 4096], P(('dp', 'tensor')), may hold values from -1.2 to 1.2
- row_order: int32 [32, 512], P('dp'), may hold values from 0 to 511, each once within a row
- out_weight: bfloat16 [2048, 4096], P('tensor'), may hold values from -0.125 to 0.125
Outputs:
- weight_grad: float32 [2048, 4096], P('tensor', 'dp')
- context_grad: bfloat16 [16384, 2048], P('dp', 'tensor')
Inputs may be any that keep to these rules, and one draw needn't show every extreme that they name: Each row of row_order is a permutation of 0 to 511.
All inputs are finite; a program needn't handle non-finite values.
Results may differ from a plain program's by a relative error of at most 0.0045.
Values may be sent and summed in bfloat16 or wider, within the bound.
A program may use at most 64 MiB of HBM per device.

v0:
```python
import jax
import jax.numpy as jnp
from jax import lax
from jax.sharding import PartitionSpec as P

EPS = 1e-06


def from_partner(value, axis, bit):
    mask = 2**bit
    pairs = [(source, source ^ mask) for source in range(lax.axis_size(axis))]
    return lax.ppermute(value, axis, pairs)


def combine_pair(first, second, s_ab, s_aa, s_bb):
    left = 1.0 - s_ab / (2.0 * (s_aa + EPS))
    right = 1.0 - s_ab / (2.0 * (s_bb + EPS))
    return left * first + right * second


def body(context, cotangent, row_order, out_weight):
    gathered = lax.all_gather(cotangent, "tensor", axis=0, tiled=True)
    used = jnp.take(gathered, row_order[0], axis=0)
    local = jnp.einsum("rk,rd->kd", context, used, preferred_element_type=jnp.float32)
    back = jnp.einsum("rd,kd->rk", used, out_weight, preferred_element_type=jnp.float32).astype(
        jnp.bfloat16
    )
    count = lax.axis_size("dp")
    levels = count.bit_length() - 1
    width = local.shape[1] // count
    index = lax.axis_index("dp")
    vector = local
    for level in range(levels):
        other = from_partner(vector, "dp", level)
        s_ab, s_aa, s_bb = lax.psum(
            (jnp.sum(vector * other), jnp.sum(vector * vector), jnp.sum(other * other)), "tensor"
        )
        vector = combine_pair(vector, other, s_ab, s_aa, s_bb)
    result = lax.dynamic_slice_in_dim(vector, index * width, width, 1)
    return (result, back)


def solution(mesh):
    in_specs = (P("dp", "tensor"), P(("dp", "tensor"), None), P("dp", None), P("tensor", None))
    out_specs = (P("tensor", "dp"), P("dp", "tensor"))
    return jax.shard_map(body, mesh=mesh, in_specs=in_specs, out_specs=out_specs, check_vma=False)
```

profile of v0, /device:TPU:1, one launch (start us, length us, event | category | flops | bytes accessed | tf_op | source)
XLA Modules:
  0.0 832.7 jit_solution(2820924414723536594)
XLA Ops:
  7.2 0.0 copy-start
  7.2 0.0 all-gather.2.cloned.1.call-start
  7.2 0.7 all-gather.2.cloned.1.call-update
  7.9 0.7 compare_select_fusion
  8.6 0.7 compare_and_fusion
  9.3 0.0 copy-start.9
  9.3 39.5 %all-gather.2.cloned.1.call-done = bf16[512,4096]{1,0:T(8,128)(2,1)} async-done(((bf16[64,4096]{1,0:T(8,128)(2,1)}), bf16[512,4096]{1,0:T(8,128)(2,1)}) %all-gather.2.cloned.1.call-update) | async-done | bytes 4194320 | tf_op jit(solution)/shard_map/all_gather | solution.py:22
  48.8 11.3 %gather_fusion = bf16[512,4096]{1,0:T(8,128)(2,1)} fusion(bf16[512,4096]{1,0:T(8,128)(2,1)} %all-gather.2.cloned.1.call-done, s32[1024]{0:T(1024)S(1)} %pad_clamp_fusion), kind=kCustom, calls=%fused_computation | custom fusion | bytes 8390656 | tf_op jit(solution)/shard_map/jit(_take)/gather | solution.py:23
  60.1 0.0 copy-done.9
  60.1 3.6 convolution_bitcast_fusion
  63.7 0.0 copy-start.4
  63.7 1.4 collective-permute-start
  65.1 90.6 %collective-permute-done = f32[256,4096]{0,1:T(8,128)S(1)} collective-permute-done((f32[256,4096]{0,1:T(8,128)S(1)}, f32[256,4096]{0,1:T(8,128)S(1)}, u32[]{:S(2)}, u32[]{:S(2)}) %collective-permute-start) | collective-permute-done | bytes 4194336 | tf_op jit(solution)/shard_map/ppermute | solution.py:12
  155.7 0.0 copy-start.5
  155.7 2.2 multiply_reduce_fusion.13
  158.0 0.0 copy-done.4
  158.0 0.0 copy-done.5
  158.0 13.5 %all-reduce.4 = (f32[]{:T(128)}, f32[]{:T(128)}, f32[]{:T(128)}) all-reduce(f32[]{:T(128)} %get-tuple-element.19, f32[]{:T(128)} %get-tuple-element.20, f32[]{:T(128)} %get-tuple-element.18), channel_id=1, replica_groups=mesh['dp'=32,'tensor'=8] {'tensor'}, use_global_device_ids=true, to_apply=%region_1.2 | all-reduce | flops 3 | bytes 24 | tf_op jit(solution)/shard_map/psum | solution.py:35
  174.1 4.0 multiply_add_fusion.3
  178.1 0.0 copy-start.1
  178.2 2.4 collective-permute-start.1
  180.5 180.0 %collective-permute-done.1 = f32[256,4096]{0,1:T(8,128)S(1)} collective-permute-done((f32[256,4096]{0,1:T(8,128)S(1)}, f32[256,4096]{0,1:T(8,128)S(1)}, u32[]{:S(2)}, u32[]{:S(2)}) %collective-permute-start.1) | collective-permute-done | bytes 4194336 | tf_op jit(solution)/shard_map/ppermute | solution.py:12
  360.5 0.0 copy-start.6
  360.5 2.2 multiply_reduce_fusion.10
  362.8 0.0 copy-done.1
  362.8 0.0 copy-done.6
  362.8 14.0 %all-reduce.3 = (f32[]{:T(128)}, f32[]{:T(128)}, f32[]{:T(128)}) all-reduce(f32[]{:T(128)} %get-tuple-element.16, f32[]{:T(128)} %get-tuple-element.17, f32[]{:T(128)} %get-tuple-element.15), channel_id=1, replica_groups=mesh['dp'=32,'tensor'=8] {'tensor'}, use_global_device_ids=true, to_apply=%region_7.8 | all-reduce | flops 3 | bytes 24 | tf_op jit(solution)/shard_map/psum | solution.py:35
  379.4 4.0 multiply_add_fusion.2
  383.4 0.0 copy-start.2
  383.4 5.7 collective-permute-start.2
  389.1 180.8 %collective-permute-done.2 = f32[256,4096]{0,1:T(8,128)S(1)} collective-permute-done((f32[256,4096]{0,1:T(8,128)S(1)}, f32[256,4096]{0,1:T(8,128)S(1)}, u32[]{:S(2)}, u32[]{:S(2)}) %collective-permute-start.2) | collective-permute-done | bytes 4194336 | tf_op jit(solution)/shard_map/ppermute | solution.py:12
  570.0 0.0 copy-start.7
  570.0 2.2 multiply_reduce_fusion.7
  572.2 0.0 copy-done.2
  572.2 0.0 copy-done.7
  572.2 13.9 %all-reduce.2 = (f32[]{:T(128)}, f32[]{:T(128)}, f32[]{:T(128)}) all-reduce(f32[]{:T(128)} %get-tuple-element.13, f32[]{:T(128)} %get-tuple-element.14, f32[]{:T(128)} %get-tuple-element.12), channel_id=1, replica_groups=mesh['dp'=32,'tensor'=8] {'tensor'}, use_global_device_ids=true, to_apply=%region_13.14 | all-reduce | flops 3 | bytes 24 | tf_op jit(solution)/shard_map/psum | solution.py:35
  588.8 4.0 multiply_add_fusion.1
  592.8 0.0 copy-start.3
  592.8 1.3 collective-permute-start.3
  594.1 90.3 %collective-permute-done.3 = f32[256,4096]{0,1:T(8,128)S(1)} collective-permute-done((f32[256,4096]{0,1:T(8,128)S(1)}, f32[256,4096]{0,1:T(8,128)S(1)}, u32[]{:S(2)}, u32[]{:S(2)}) %collective-permute-start.3) | collective-permute-done | bytes 4194336 | tf_op jit(solution)/shard_map/ppermute | solution.py:12
  684.4 0.0 copy-start.8
  684.4 2.2 multiply_reduce_fusion.4
  686.6 0.0 copy-done.3
  686.6 0.0 copy-done.8
  686.6 13.9 %all-reduce.1 = (f32[]{:T(128)}, f32[]{:T(128)}, f32[]{:T(128)}) all-reduce(f32[]{:T(128)} %get-tuple-element.10, f32[]{:T(128)} %get-tuple-element.11, f32[]{:T(128)} %get-tuple-element.9), channel_id=1, replica_groups=mesh['dp'=32,'tensor'=8] {'tensor'}, use_global_device_ids=true, to_apply=%region_19.20 | all-reduce | flops 3 | bytes 24 | tf_op jit(solution)/shard_map/psum | solution.py:35
  703.1 6.0 multiply_add_fusion
  709.1 2.7 collective-permute-start.4
  711.8 0.0 copy-done
  711.8 4.2 fusion.1
  716.0 86.4 %collective-permute-done.4 = f32[256,4096]{0,1:T(8,128)} collective-permute-done((f32[256,4096]{0,1:T(8,128)}, f32[256,4096]{0,1:T(8,128)}, u32[]{:S(2)}, u32[]{:S(2)}) %collective-permute-start.4) | collective-permute-done | bytes 4194336 | tf_op jit(solution)/shard_map/ppermute | solution.py:12
  802.4 5.2 multiply_reduce_fusion.1
  807.6 14.0 %all-reduce = (f32[]{:T(128)}, f32[]{:T(128)}, f32[]{:T(128)}) all-reduce(f32[]{:T(128)} %get-tuple-element.7, f32[]{:T(128)} %get-tuple-element.8, f32[]{:T(128)} %get-tuple-element.6), channel_id=1, replica_groups=mesh['dp'=32,'tensor'=8] {'tensor'}, use_global_device_ids=true, to_apply=%region_25.26 | all-reduce | flops 3 | bytes 24 | tf_op jit(solution)/shard_map/psum | solution.py:35
  824.1 1.0 fusion.2
  825.1 0.8 copy.7
  (1 shorter events, 0.0 us)
Async XLA Ops:
  7.2 704.7 %copy-start = (bf16[256,4096]{1,0:T(8,128)(2,1)S(1)}, bf16[256,4096]{1,0:T(8,128)(2,1)}, u32[]{:S(2)}) copy-start(bf16[256,4096]{1,0:T(8,128)(2,1)} %param.7) | copy-start | bytes 6291460
  7.2 41.6 %all-gather.2.cloned.1.call-start = ((), (), s32[]{:S(2)}) async-start(), calls=%async_computation | async-start | bytes 4718592 | tf_op jit(solution)/shard_map/all_gather | solution.py:22
  9.3 50.8 %copy-start.9 = (bf16[512,256]{1,0:T(8,128)(2,1)S(1)}, bf16[512,256]{1,0:T(8,128)(2,1)}, u32[]{:S(2)}) copy-start(bf16[512,256]{1,0:T(8,128)(2,1)} %param.4) | copy-start | bytes 786436
  63.7 94.3 %copy-start.4 = (f32[256,4096]{0,1:T(8,128)}, f32[256,4096]{0,1:T(8,128)S(1)}, u32[]{:S(2)}) copy-start(f32[256,4096]{0,1:T(8,128)S(1)} %convolution_bitcast_fusion) | copy-start | bytes 12582916
  63.7 92.0 %collective-permute-start = (f32[256,4096]{0,1:T(8,128)S(1)}, f32[256,4096]{0,1:T(8,128)S(1)}, u32[]{:S(2)}, u32[]{:S(2)}) collective-permute-start(f32[256,4096]{0,1:T(8,128)S(1)} %convolution_bitcast_fusion), channel_id=1, source_target_pairs={{0,8},{8,0},{16,24},{24,16},{32,40},{40,32},{48,56},{56,48},{64,72... | collective-permute-start | bytes 12582920 | tf_op jit(solution)/shard_map/ppermute | solution.py:12
  155.7 2.3 copy-start.5
  178.1 184.6 %copy-start.1 = (f32[256,4096]{0,1:T(8,128)}, f32[256,4096]{0,1:T(8,128)S(1)}, u32[]{:S(2)}) copy-start(f32[256,4096]{0,1:T(8,128)S(1)} %multiply_add_fusion.3) | copy-start | bytes 12582916
  178.2 182.4 %collective-permute-start.1 = (f32[256,4096]{0,1:T(8,128)S(1)}, f32[256,4096]{0,1:T(8,128)S(1)}, u32[]{:S(2)}, u32[]{:S(2)}) collective-permute-start(f32[256,4096]{0,1:T(8,128)S(1)} %multiply_add_fusion.3), channel_id=1, source_target_pairs={{0,16},{8,24},{16,0},{24,8},{32,48},{40,56},{48,32},{56,40},{64,80... | collective-permute-start | bytes 12582920 | tf_op jit(solution)/shard_map/ppermute | solution.py:12
  360.5 2.3 copy-start.6
  383.4 188.8 %copy-start.2 = (f32[256,4096]{0,1:T(8,128)}, f32[256,4096]{0,1:T(8,128)S(1)}, u32[]{:S(2)}) copy-start(f32[256,4096]{0,1:T(8,128)S(1)} %multiply_add_fusion.2) | copy-start | bytes 12582916
  383.4 186.6 %collective-permute-start.2 = (f32[256,4096]{0,1:T(8,128)S(1)}, f32[256,4096]{0,1:T(8,128)S(1)}, u32[]{:S(2)}, u32[]{:S(2)}) collective-permute-start(f32[256,4096]{0,1:T(8,128)S(1)} %multiply_add_fusion.2), channel_id=1, source_target_pairs={{0,32},{8,40},{16,48},{24,56},{32,0},{40,8},{48,16},{56,24},{64,96... | collective-permute-start | bytes 12582920 | tf_op jit(solution)/shard_map/ppermute | solution.py:12
  570.0 2.3 copy-start.7
  592.8 93.8 %copy-start.3 = (f32[256,4096]{0,1:T(8,128)}, f32[256,4096]{0,1:T(8,128)S(1)}, u32[]{:S(2)}) copy-start(f32[256,4096]{0,1:T(8,128)S(1)} %multiply_add_fusion.1) | copy-start | bytes 12582916
  592.8 91.6 %collective-permute-start.3 = (f32[256,4096]{0,1:T(8,128)S(1)}, f32[256,4096]{0,1:T(8,128)S(1)}, u32[]{:S(2)}, u32[]{:S(2)}) collective-permute-start(f32[256,4096]{0,1:T(8,128)S(1)} %multiply_add_fusion.1), channel_id=1, source_target_pairs={{0,64},{8,72},{16,80},{24,88},{32,96},{40,104},{48,112},{56,120},{... | collective-permute-start | bytes 12582920 | tf_op jit(solution)/shard_map/ppermute | solution.py:12
  684.4 2.2 copy-start.8
  709.1 93.3 %collective-permute-start.4 = (f32[256,4096]{0,1:T(8,128)}, f32[256,4096]{0,1:T(8,128)}, u32[]{:S(2)}, u32[]{:S(2)}) collective-permute-start(f32[256,4096]{0,1:T(8,128)} %multiply_add_fusion), channel_id=1, source_target_pairs={{0,128},{8,136},{16,144},{24,152},{32,160},{40,168},{48,176},{56,1... | collective-permute-start | bytes 12582920 | tf_op jit(solution)/shard_map/ppermute | solution.py:12
Sparse Core Ops, SparseCore 0:
  9.9 38.8 all-gather.1
where the time goes:
time: 833 us
  waiting for transfers between devices  668 us (80%)
  blocking collectives  69.3 us (8%)
  other arithmetic  34.6 us (4%)
  between operations  27.1 us (3%)
  starting transfers between devices  13.5 us (2%)
  local copies, waits for them, and re-layouts  12.1 us (1%)
    ppermute x5, waiting for transfers between devices, from_partner(): return lax.ppermute(value, axis, pairs)  628 us
    psum x5, blocking collectives, body(): lax.psum((jnp.sum(vector * other), jnp.sum(vector * vector), jnp.sum(othe...  69.3 us
    all_gather x1, waiting for transfers between devices, body(): gathered = lax.all_gather(cotangent, 'tensor', axis=0, tiled=True)  39.5 us
    add x5, other arithmetic, combine_pair(): return left * first + right * second  19 us
  transfers between devices with their start and end apart: 6, of which 6 were waited for; matrix products, arithmetic and copies ran while one was open for 1% of the time, Pallas kernels for 0%

commit v1 on v0

v1 whole, which is shorter than its diff:
```python
import jax
import jax.numpy as jnp
from jax import lax
from jax.experimental import pallas as pl
from jax.experimental.pallas import tpu as pltpu
from jax.sharding import PartitionSpec as P

EPS = 1e-06
MESH = pl.DeviceIdType.MESH
BF16, F32 = jnp.bfloat16, jnp.float32
NY, NZ, NX, NC = 4, 8, 4, 2
ROWS, SHARD = 512, 64
HEADS, D = 256, 4096
SLICE = D // NZ
WIDE = D // (NY * NZ)
HALF = HEADS // 2
N_DP = NY * NZ
PEERS_A = [(dz, dc) for dz in (4, 3, 5, 2, 6, 1, 7, 0) for dc in (1, 0) if dz or dc]
PEERS_B = [(dy, dx) for dy, dx in sorted(((a, b) for a in range(NY) for b in range(NX)), key=lambda p: -min(p[0], NY - p[0]) - min(p[1], NX - p[1])) if dy or dx]
ORDER = (0, 1, 7, 2, 6, 3, 5, 4)


def kernel(
    context, cotangent, row_order, out_weight, out_grad, out_back,
    uf, us, pack, ct, cv, ov, wv, pt, gst, gv, acc, src_a, src_b, in_a, in_b, wts,
    local, us_s, us_r, aa_s, aa_r, uf_s, uf_r, ct_s, ct_r, gv_s, gv_r, a_s, a_r, b_s, b_r,
):
    dp, tp = lax.axis_index("dp"), lax.axis_index("tensor")
    y, z = lax.div(dp, NZ), lax.rem(dp, NZ)
    x, c = lax.div(tp, NC), lax.rem(tp, NC)

    def device(dy=0, dz=0, dx=0, dc=0):
        return (
            lax.rem(y + dy, NY) * NZ + lax.rem(z + dz, NZ),
            lax.rem(x + dx, NX) * NC + lax.rem(c + dc, NC),
        )

    started = []

    def send(source, target, send_sem, recv_sem, where):
        copy = pltpu.make_async_remote_copy(
            src_ref=source, dst_ref=target, send_sem=send_sem, recv_sem=recv_sem,
            device_id=where, device_id_type=MESH,
        )
        copy.start()
        started.append(copy)
        return copy

    barrier = pltpu.get_barrier_semaphore()
    for dz, dc in PEERS_A:
        pl.semaphore_signal(barrier, inc=1, device_id=device(dz=dz, dc=dc), device_id_type=MESH)
    for dy, dx in PEERS_B:
        pl.semaphore_signal(barrier, inc=1, device_id=device(dy=dy, dx=dx), device_id_type=MESH)

    load_cot = pltpu.make_async_copy(cotangent, uf.at[c, x], local.at[0])
    load_ctx = pltpu.make_async_copy(context, cv, local.at[1])
    load_ord = pltpu.make_async_copy(row_order, ov, local.at[2])
    load_w = pltpu.make_async_copy(out_weight, wv, local.at[3])
    load_cot.start()
    load_ctx.start()
    load_ord.start()
    load_w.start()

    load_cot.wait()
    for d in range(NZ):
        to = lax.rem(z + d, NZ)
        for j in range(NY):
            at = pl.multiple_of((j * NZ + to) * WIDE, WIDE)
            block = uf[c, x, :, pl.ds(at, WIDE)]
            if d == 0:
                us[0, c, x, :, j * WIDE : (j + 1) * WIDE] = block
            else:
                pack[d - 1, :, j * WIDE : (j + 1) * WIDE] = block
    pl.semaphore_wait(barrier, len(PEERS_A) + len(PEERS_B))

    right, left, sibling = device(dx=1), device(dx=NX - 1), device(dc=1)
    xl, xr, xf = lax.rem(x + NX - 1, NX), lax.rem(x + 1, NX), lax.rem(x + 2, NX)
    lo, hi = pl.ds(0, SHARD // 2), pl.ds(SHARD // 2, SHARD // 2)
    copies = {}

    def us_own(d):
        mine = us.at[d, c, x]
        copies["us", d, 0] = send(mine, mine, us_s.at[d, 0], us_r.at[d, 0], right)
        copies["us", d, 1] = send(mine, mine, us_s.at[d, 1], us_r.at[d, 1], left)

    def us_forward(d):
        copies["us", d, 0].wait_recv()
        part = us.at[d, c, xl, lo]
        copies["us", d, 2] = send(part, part, us_s.at[d, 2], us_r.at[d, 2], right)
        copies["us", d, 1].wait_recv()
        part = us.at[d, c, xr, hi]
        copies["us", d, 3] = send(part, part, us_s.at[d, 3], us_r.at[d, 3], left)

    def us_share(d):
        copies["us", d, 2].wait_recv()
        copies["us", d, 3].wait_recv()
        part = us.at[d, c]
        copies["us", d, 4] = send(part, part, us_s.at[d, 4], us_r.at[d, 4], sibling)

    def uf_own():
        for k, (rows, to) in enumerate(((lo, right), (hi, left), (hi, right), (lo, left))):
            part = uf.at[c, x, rows]
            copies["uf", k] = send(part, part, uf_s.at[k], uf_r.at[k], to)
        part = uf.at[c, x]
        copies["uf", 6] = send(part, part, uf_s.at[6], uf_r.at[6], sibling)

    def uf_forward():
        copies["uf", 0].wait_recv()
        part = uf.at[c, xl, lo]
        copies["uf", 4] = send(part, part, uf_s.at[4], uf_r.at[4], right)
        copies["uf", 1].wait_recv()
        part = uf.at[c, xr, hi]
        copies["uf", 5] = send(part, part, uf_s.at[5], uf_r.at[5], left)

    def uf_share():
        copies["uf", 2].wait_recv()
        part = uf.at[c, xl]
        copies["uf", 7] = send(part, part, uf_s.at[7], uf_r.at[7], sibling)
        copies["uf", 3].wait_recv()
        part = uf.at[c, xr]
        copies["uf", 8] = send(part, part, uf_s.at[8], uf_r.at[8], sibling)
        copies["uf", 4].wait_recv()
        copies["uf", 5].wait_recv()
        part = uf.at[c, xf]
        copies["uf", 9] = send(part, part, uf_s.at[9], uf_r.at[9], sibling)

    def ct_send(slot, h, step):
        to = (slot - step) % NZ
        copies["ct", to, h] = send(
            ct.at[slot, h], ct.at[to, h], ct_s.at[to, h], ct_r.at[to, h], device(dz=step % NZ)
        )

    def ct_arrived(d):
        for h in range(2):
            copies["ct", d, h].wait_recv()
            if d in (7, 6) or (d == 5 and h == 0):
                ct_send(d, h, 1)
            if d in (1, 2) or (d == 3 and h == 1):
                ct_send(d, h, -1)

    def replica(d, e=0):
        return lax.rem(y + e, NY) * NZ + lax.rem(z + d, NZ)

    def gradient(d, h):
        value = jnp.dot(ct[d, h], us[d].reshape(ROWS, SLICE), preferred_element_type=F32).astype(BF16)
        for j in range(NY):
            gst[d, h, j] = value[:, j * WIDE : (j + 1) * WIDE]
        b = replica(d)
        target = gv.at[b, pl.ds(h * HALF, HALF)]
        for e in (2, 1, 3):
            copies["gv", d, h, e] = send(
                gst.at[d, h, lax.rem(y + e, NY)], target, gv_s.at[d, h, e - 1], gv_r.at[d, h, e - 1], device(dy=e)
            )
        gv[b, h * HALF : (h + 1) * HALF] = gst[d, h, y]

    def gram_pair(d1, d2):
        first = [replica(d1, e) for e in range(NY)]
        second = [replica(d2, e) for e in range(NY)]
        pairs = [(i, j) for i in range(NY) for j in range(NY) if d1 != d2 or i <= j]

        def body(step, sums):
            at = pl.ds(pl.multiple_of(step * 16, 16), 16)
            a = [gv[b, at].astype(F32) for b in first]
            bs = a if d1 == d2 else [gv[b, at].astype(F32) for b in second]
            return tuple(s + a[i] * bs[j] for s, (i, j) in zip(sums, pairs))

        sums = lax.fori_loop(0, HEADS // 16, body, tuple(jnp.zeros((16, WIDE), F32) for _ in pairs))
        for s, (i, j) in zip(sums, pairs):
            line = jnp.sum(s, axis=0, keepdims=True)
            zi, yi = lax.rem(z + d1, NZ), lax.rem(y + i, NY)
            zj, yj = lax.rem(z + d2, NZ), lax.rem(y + j, NY)
            acc[pl.ds(zi * 128 + yi * N_DP + yj * NZ + zj, 1), :] = line
            acc[pl.ds(zj * 128 + yj * N_DP + yi * NZ + zi, 1), :] = line

    done = []

    def gram(d):
        for h in range(2):
            for e in (1, 3, 2):
                copies["gv", d, h, e].wait_recv()
        done.append(d)
        for other in done:
            gram_pair(d, other)

    us_own(0)
    for d in ORDER[1:]:
        copies["aa", NZ - d] = send(
            pack.at[d - 1], us.at[NZ - d, c, x], aa_s.at[NZ - d], aa_r.at[NZ - d], device(dz=d)
        )

    load_ctx.wait()
    load_ord.wait()
    row = lax.broadcasted_iota(jnp.int32, (ROWS, ROWS), 0)
    name = lax.rem(lax.div(row, SHARD), NX) * (NC * SHARD) + lax.div(row, NX * SHARD) * SHARD + lax.rem(row, SHARD)
    pt[...] = (ov[...] == name).astype(F32).astype(BF16)
    mine = lax.dot_general(cv[...], pt[...], (((0,), (1,)), ((), ())), preferred_element_type=F32).astype(BF16)
    ct[0, 0] = mine[:HALF]
    ct[0, 1] = mine[HALF:]
    for h in range(2):
        ct_send(0, h, 1)
        ct_send(0, h, -1)

    us_forward(0)
    for d in (1, 7):
        copies["aa", d].wait_recv()
        us_own(d)
    us_share(0)
    for d in (1, 7):
        us_forward(d)
    for d in (2, 6):
        copies["aa", d].wait_recv()
        us_own(d)
    copies["us", 0, 4].wait_recv()
    gradient(0, 0)
    gradient(0, 1)
    for d in (1, 7):
        us_share(d)
    ct_arrived(7)
    ct_arrived(1)
    for d in (2, 6):
        us_forward(d)
    for d in (3, 5, 4):
        copies["aa", d].wait_recv()
        us_own(d)
    for d in (1, 7):
        copies["us", d, 4].wait_recv()
        gradient(d, 0)
        gradient(d, 1)
    for d in (2, 6):
        us_share(d)
    for d in (3, 5, 4):
        us_forward(d)
    gram(0)
    ct_arrived(6)
    ct_arrived(2)
    for d in (3, 5, 4):
        us_share(d)
    uf_own()
    for d in (2, 6):
        copies["us", d, 4].wait_recv()
        gradient(d, 0)
        gradient(d, 1)
    gram(1)
    gram(7)
    ct_arrived(5)
    ct_arrived(3)
    for d in (3, 5):
        copies["us", d, 4].wait_recv()
        gradient(d, 0)
        gradient(d, 1)
    gram(2)
    gram(6)
    uf_forward()
    ct_arrived(4)
    copies["us", 4, 4].wait_recv()
    gradient(4, 0)
    gradient(4, 1)
    gram(3)
    gram(5)
    gram(4)

    ones = jnp.ones((8, 128), BF16)
    sums = acc[...]
    high = sums.astype(BF16)
    low = (sums - high.astype(F32)).astype(BF16)
    over_lanes = (((1,), (1,)), ((), ()))
    flat = lax.dot_general(ones, high, over_lanes, preferred_element_type=F32) + lax.dot_general(
        ones, low, over_lanes, preferred_element_type=F32
    )
    sub = lax.broadcasted_iota(jnp.int32, (8, 128), 0)
    tile = jnp.zeros((8, 128), F32)
    for i in range(8):
        tile = jnp.where(sub == i, flat[:, i * 128 : (i + 1) * 128], tile)
    src_a[...] = tile
    stage_a = [
        send(src_a, in_a.at[k], a_s.at[k], a_r.at[k], device(dz=dz, dc=dc)) for k, (dz, dc) in enumerate(PEERS_A)
    ]

    uf_share()
    load_w.wait()
    for k in range(6, 10):
        copies["uf", k].wait_recv()
    over_width = (((1,), (1,)), ((), ()))
    parts = []
    for core in range(NC):
        rows = uf[core].reshape(NX * SHARD, D)
        parts.append(
            lax.dot_general(rows, wv[...], over_width, preferred_element_type=F32).astype(BF16)
        )
    gathered = jnp.concatenate(parts, axis=0)
    out_back[...] = lax.dot_general(pt[...], gathered, (((0,), (0,)), ((), ())), preferred_element_type=F32).astype(BF16)

    total = src_a[...]
    for k, copy in enumerate(stage_a):
        copy.wait_recv()
        total = total + in_a[k]
    src_b[...] = total
    stage_b = [
        send(src_b, in_b.at[k], b_s.at[k], b_r.at[k], device(dy=dy, dx=dx)) for k, (dy, dx) in enumerate(PEERS_B)
    ]
    for k, copy in enumerate(stage_b):
        copy.wait_recv()
        total = total + in_b[k]

    quarter = [total] + [pltpu.roll(total, 128 - N_DP * q, 1) for q in range(1, NY)]
    m = jnp.concatenate(quarter, axis=0)
    row = lax.broadcasted_iota(jnp.int32, (N_DP, 128), 0)
    lane = lax.broadcasted_iota(jnp.int32, (N_DP, 128), 1)
    m = jnp.where(lane < N_DP, m, 0.0)
    weight = jnp.ones((N_DP, 1), F32)
    for level in range(5):
        bit = 1 << level
        own = jnp.where(lane == row, m, 0.0)
        mixed = jnp.where(lane == (row ^ bit), m, 0.0)
        down = 1.0 - jnp.sum(mixed, axis=1, keepdims=True) / (2.0 * (jnp.sum(own, axis=1, keepdims=True) + EPS))
        across = 1.0 - jnp.sum(mixed, axis=0, keepdims=True) / (2.0 * (jnp.sum(own, axis=0, keepdims=True) + EPS))
        weight = weight * down
        m = (down * across) * m
        m = m + jnp.where((row & bit) == 0, pltpu.roll(m, N_DP - bit, 0), pltpu.roll(m, bit, 0))
        m = m + jnp.where((lane & bit) == 0, pltpu.roll(m, 128 - bit, 1), pltpu.roll(m, bit, 1))
        m = jnp.where(lane < N_DP, m, 0.0)
    wts[...] = jnp.broadcast_to(weight, (N_DP, 128))

    def combine(step, _):
        at = pl.ds(pl.multiple_of(step * 16, 16), 16)
        value = jnp.zeros((16, WIDE), F32)
        for b in range(N_DP):
            value = value + gv[b, at].astype(F32) * wts[b : b + 1, :]
        out_grad[at, :] = value
        return 0

    lax.fori_loop(0, HEADS // 16, combine, 0)
    for copy in started:
        copy.wait_send()


def body(context, cotangent, row_order, out_weight):
    sem = pltpu.SemaphoreType.DMA
    return pl.pallas_call(
        kernel,
        out_shape=(
            jax.ShapeDtypeStruct((HEADS, WIDE), F32),
            jax.ShapeDtypeStruct((ROWS, HEADS), BF16),
        ),
        in_specs=[pl.BlockSpec(memory_space=pl.ANY)] * 4,
        out_specs=[pl.BlockSpec(memory_space=pltpu.VMEM)] * 2,
        scratch_shapes=[
            pltpu.VMEM((NC, NX, SHARD, D), BF16),
            pltpu.VMEM((NZ, NC, NX, SHARD, SLICE), BF16),
            pltpu.VMEM((NZ - 1, SHARD, SLICE), BF16),
            pltpu.VMEM((NZ, 2, HALF, ROWS), BF16),
            pltpu.VMEM((ROWS, HEADS), BF16),
            pltpu.VMEM((1, ROWS), jnp.int32),
            pltpu.VMEM((HEADS, D), BF16),
            pltpu.VMEM((ROWS, ROWS), BF16),
            pltpu.VMEM((NZ, 2, NY, HALF, WIDE), BF16),
            pltpu.VMEM((N_DP, HEADS, WIDE), BF16),
            pltpu.VMEM((N_DP * N_DP, 128), F32),
            pltpu.VMEM((8, 128), F32),
            pltpu.VMEM((8, 128), F32),
            pltpu.VMEM((len(PEERS_A), 8, 128), F32),
            pltpu.VMEM((len(PEERS_B), 8, 128), F32),
            pltpu.VMEM((N_DP, 128), F32),
            sem((4,)),
            sem((NZ, 5)),
            sem((NZ, 5)),
            sem((NZ,)),
            sem((NZ,)),
            sem((10,)),
            sem((10,)),
            sem((NZ, 2)),
            sem((NZ, 2)),
            sem((NZ, 2, NY - 1)),
            sem((NZ, 2, NY - 1)),
            sem((len(PEERS_A),)),
            sem((len(PEERS_A),)),
            sem((len(PEERS_B),)),
            sem((len(PEERS_B),)),
        ],
        name="adasum",
        compiler_params=pltpu.CompilerParams(
            collective_id=0, has_side_effects=True, vmem_limit_bytes=48 << 20
        ),
        cost_estimate=pl.CostEstimate(flops=2_300_000_000, bytes_accessed=4_000_000, transcendentals=0),
    )(context, cotangent, row_order, out_weight)


def solution(mesh):
    in_specs = (P("dp", "tensor"), P(("dp", "tensor"), None), P("dp", None), P("tensor", None))
    out_specs = (P("tensor", "dp"), P("dp", "tensor"))
    return jax.shard_map(body, mesh=mesh, in_specs=in_specs, out_specs=out_specs, check_vma=False)
```

time: 833 us -> 82.1 us (0.10)
  waiting for transfers between devices: 668 us -> 0 us
  Pallas kernels: 0 us -> 75.6 us
  blocking collectives: 69.3 us -> 0 us
  other arithmetic: 34.6 us -> 0 us
  between operations: 27.1 us -> 0.65 us
  starting transfers between devices: 13.5 us -> 0 us
    ppermute x5 -> x0, waiting for transfers between devices: 628 us -> none  [from_partner(): return lax.ppermute(value, axis, pairs)]
    pallas_call x0 -> x1, Pallas kernels: none -> 75.6 us  [body(): pl.pallas_call(kernel, out_shape=(jax.ShapeDtypeStruct((HEADS, WIDE), F32...]
    psum x5 -> x0, blocking collectives: 69.3 us -> none  [body(): lax.psum((jnp.sum(vector * other), jnp.sum(vector * vector), jnp.sum(othe...]
    all_gather x1 -> x0, waiting for transfers between devices: 39.5 us -> none  [body(): gathered = lax.all_gather(cotangent, 'tensor', axis=0, tiled=True)]
    add x5 -> x0, other arithmetic: 19 us -> none  [combine_pair(): return left * first + right * second]
    reduce_sum x5 -> x0, other arithmetic: 14.2 us -> none  [body(): jnp.sum(vector * vector)]
    ppermute x5 -> x0, starting transfers between devices: 13.5 us -> none  [from_partner(): return lax.ppermute(value, axis, pairs)]
    gather x1 -> x0, local copies, waits for them, and re-layouts: 11.3 us -> none  [body(): used = jnp.take(gathered, row_order[0], axis=0)]
  transfers between devices with their start and end apart: 6 -> 0, of which waited for: 6 -> 0; matrix products, arithmetic and copies ran while one was open for 1% -> 0% of each run, Pallas kernels for 0% -> 0%
where the time goes in v1:
time: 82.1 us; the launch traced here: 81.9 us
  Pallas kernels  75.6 us (92%)
  local copies, waits for them, and re-layouts  5.62 us (7%)
    pallas_call x1, Pallas kernels, body(): pl.pallas_call(kernel, out_shape=(jax.ShapeDtypeStruct((HEADS, WIDE), F32...  75.6 us
    unnamed x10, local copies, waits for them, and re-layouts  5.62 us

profile of v1, /device:TPU:1, one launch (start us, length us, event | category | flops | bytes accessed | tf_op | source)
XLA Modules:
  0.0 81.9 jit_solution(9983529184041383506)
XLA Ops:
  0.6 0.0 copy-start
  0.6 1.6 %copy-done = bf16[256,4096]{1,0:T(8,128)(2,1)S(1)} copy-done((bf16[256,4096]{1,0:T(8,128)(2,1)S(1)}, bf16[256,4096]{1,0:T(8,128)(2,1)}, u32[]{:S(2)}) %copy-start) | copy-done | bytes 2097176
  2.2 0.0 copy-start.1
  2.2 1.0 %copy-done.1 = bf16[64,4096]{1,0:T(8,128)(2,1)S(1)} copy-done((bf16[64,4096]{1,0:T(8,128)(2,1)S(1)}, bf16[64,4096]{1,0:T(8,128)(2,1)}, u32[]{:S(2)}) %copy-start.1) | copy-done | bytes 524312
  3.3 0.0 copy-start.2
  3.3 0.9 %copy-done.2 = bf16[512,256]{1,0:T(8,128)(2,1)S(1)} copy-done((bf16[512,256]{1,0:T(8,128)(2,1)S(1)}, bf16[512,256]{1,0:T(8,128)(2,1)}, u32[]{:S(2)}) %copy-start.2) | copy-done | bytes 262168
  4.2 0.0 copy-start.3
  4.2 0.7 copy-done.3
  4.9 75.6 %adasum.1 = (f32[256,128]{1,0:T(8,128)S(1)}, bf16[512,256]{1,0:T(8,128)(2,1)S(1)}) custom-call(bf16[512,256]{1,0:T(8,128)(2,1)S(1)} %copy-done.2, bf16[64,4096]{1,0:T(8,128)(2,1)S(1)} %copy-done.1, s32[1,512]{1,0:T(1,128)S(1)} %copy-done.3, bf16[256,4096]{1,0:T(8,128)(2,1)S(1)} %copy-done), custom_call_target="tpu_custom_call" | custom-call | flops 2300000000 | bytes 4000000 | tf_op jit(solution)/shard_map/adasum/pallas_call | solution.py:339
  80.5 0.7 copy.8
  81.2 0.7 copy.9
Async XLA Ops:
  0.6 1.6 %copy-start = (bf16[256,4096]{1,0:T(8,128)(2,1)S(1)}, bf16[256,4096]{1,0:T(8,128)(2,1)}, u32[]{:S(2)}) copy-start(bf16[256,4096]{1,0:T(8,128)(2,1)} %out_weight.1) | copy-start | bytes 6291460
  2.2 1.0 %copy-start.1 = (bf16[64,4096]{1,0:T(8,128)(2,1)S(1)}, bf16[64,4096]{1,0:T(8,128)(2,1)}, u32[]{:S(2)}) copy-start(bf16[64,4096]{1,0:T(8,128)(2,1)} %cotangent.1) | copy-start | bytes 1572868
  3.3 0.9 %copy-start.2 = (bf16[512,256]{1,0:T(8,128)(2,1)S(1)}, bf16[512,256]{1,0:T(8,128)(2,1)}, u32[]{:S(2)}) copy-start(bf16[512,256]{1,0:T(8,128)(2,1)} %context.1) | copy-start | bytes 786436
  4.2 0.7 copy-start.3

commit v2 on v1

v2 whole, which is shorter than its diff:
```python
import jax
import jax.numpy as jnp
from jax import lax
from jax.experimental import pallas as pl
from jax.experimental.pallas import tpu as pltpu
from jax.sharding import PartitionSpec as P

EPS = 1e-06
MESH = pl.DeviceIdType.MESH
BF16, F32 = jnp.bfloat16, jnp.float32
NY, NZ, NX, NC = 4, 8, 4, 2
ROWS, SHARD = 512, 64
HEADS, D = 256, 4096
SLICE = D // NZ
WIDE = D // (NY * NZ)
HALF = HEADS // 2
N_DP = NY * NZ
PEERS_A = [(dz, dc) for dz in (4, 3, 5, 2, 6, 1, 7, 0) for dc in (1, 0) if dz or dc]
PEERS_B = [(dy, dx) for dy, dx in sorted(((a, b) for a in range(NY) for b in range(NX)), key=lambda p: -min(p[0], NY - p[0]) - min(p[1], NX - p[1])) if dy or dx]
NEIGHBOURS = [(0, dz, 0, 0) for dz in (4, 3, 5, 2, 6, 1, 7)] + [(dy, 0, 0, 0) for dy in (2, 1, 3)] + [(0, 0, dx, 0) for dx in (2, 1, 3)] + [(0, 0, 0, 1)]


def kernel(
    context, cotangent, row_order, out_weight, hbm_grad, hbm_back, out_grad, out_back,
    uf, us, pack, ct, cv, ov, wv, pt, gst, gv, acc, src_a, src_b, in_a, in_b, wts,
    local, sent, us_r, aa_r, uf_r, ct_r, gv_r, ab_r,
):
    dp, tp = lax.axis_index("dp"), lax.axis_index("tensor")
    y, z = lax.div(dp, NZ), lax.rem(dp, NZ)
    x, c = lax.div(tp, NC), lax.rem(tp, NC)

    def device(dy=0, dz=0, dx=0, dc=0):
        return (
            lax.rem(y + dy, NY) * NZ + lax.rem(z + dz, NZ),
            lax.rem(x + dx, NX) * NC + lax.rem(c + dc, NC),
        )

    def send(source, target, kind, recv_sem, where):
        pltpu.make_async_remote_copy(
            src_ref=source, dst_ref=target, send_sem=sent.at[kind], recv_sem=recv_sem,
            device_id=where, device_id_type=MESH,
        ).start()

    def wait(ref, sem):
        pltpu.make_async_copy(ref, ref, sem).wait()

    barrier = pltpu.get_barrier_semaphore()
    for step in NEIGHBOURS:
        pl.semaphore_signal(barrier, inc=1, device_id=device(*step), device_id_type=MESH)

    load_cot = pltpu.make_async_copy(cotangent, uf.at[c, x], local.at[0])
    load_ctx = pltpu.make_async_copy(context, cv, local.at[1])
    load_ord = pltpu.make_async_copy(row_order, ov, local.at[2])
    load_w = pltpu.make_async_copy(out_weight, wv, local.at[3])
    load_cot.start()
    load_ctx.start()
    load_ord.start()
    load_w.start()

    load_cot.wait()
    for d in range(NZ):
        to = lax.rem(z + d, NZ)
        for j in range(NY):
            at = pl.multiple_of((j * NZ + to) * WIDE, WIDE)
            block = uf[c, x, :, pl.ds(at, WIDE)]
            if d == 0:
                us[0, c, x, :, j * WIDE : (j + 1) * WIDE] = block
            else:
                pack[d - 1, :, j * WIDE : (j + 1) * WIDE] = block

    load_ctx.wait()
    load_ord.wait()
    row = lax.broadcasted_iota(jnp.int32, (ROWS, ROWS), 0)
    name = lax.rem(lax.div(row, SHARD), NX) * (NC * SHARD) + lax.div(row, NX * SHARD) * SHARD + lax.rem(row, SHARD)
    pt[...] = (ov[...] == name).astype(F32).astype(BF16)
    mine = lax.dot_general(cv[...], pt[...], (((0,), (1,)), ((), ())), preferred_element_type=F32).astype(BF16)
    ct[0, 0] = mine[:HALF]
    ct[0, 1] = mine[HALF:]
    pl.semaphore_wait(barrier, len(NEIGHBOURS))

    right, left, sibling = device(dx=1), device(dx=NX - 1), device(dc=1)
    xl, xr, xf = lax.rem(x + NX - 1, NX), lax.rem(x + 1, NX), lax.rem(x + 2, NX)
    lo, hi = pl.ds(0, SHARD // 2), pl.ds(SHARD // 2, SHARD // 2)

    def us_own(d):
        mine = us.at[d, c, x]
        send(mine, mine, 0, us_r.at[d, 0], right)
        send(mine, mine, 0, us_r.at[d, 0], left)

    def us_forward(d):
        wait(us.at[d, c, pl.ds(0, 2)], us_r.at[d, 0])
        part = us.at[d, c, xl, lo]
        send(part, part, 0, us_r.at[d, 1], right)
        part = us.at[d, c, xr, hi]
        send(part, part, 0, us_r.at[d, 1], left)

    def us_share(d):
        wait(us.at[d, c, 0], us_r.at[d, 1])
        part = us.at[d, c]
        send(part, part, 0, us_r.at[d, 2], sibling)

    def us_ready(d):
        wait(us.at[d, c], us_r.at[d, 2])

    def aa_send(d):
        send(pack.at[d - 1], us.at[NZ - d, c, x], 1, aa_r.at[NZ - d], device(dz=d))

    def aa_ready(d):
        wait(pack.at[0], aa_r.at[d])

    def uf_own(k):
        for rows, to in ((lo, right), (hi, left)) if k == 0 else ((hi, right), (lo, left)):
            part = uf.at[c, x, rows]
            send(part, part, 2, uf_r.at[k], to)
        if k == 0:
            part = uf.at[c, x]
            send(part, part, 2, uf_r.at[3], sibling)

    def uf_forward():
        wait(uf.at[c, x], uf_r.at[0])
        part = uf.at[c, xl, lo]
        send(part, part, 2, uf_r.at[2], right)
        part = uf.at[c, xr, hi]
        send(part, part, 2, uf_r.at[2], left)

    def uf_share():
        wait(uf.at[c, x], uf_r.at[1])
        for at in (xl, xr):
            part = uf.at[c, at]
            send(part, part, 2, uf_r.at[3], sibling)
        wait(uf.at[c, x], uf_r.at[2])
        part = uf.at[c, xf]
        send(part, part, 2, uf_r.at[3], sibling)

    def ct_send(slot, h, step):
        to = (slot - step) % NZ
        send(ct.at[slot, h], ct.at[to, h], 3, ct_r.at[to, h], device(dz=step % NZ))

    def ct_arrived(d, h):
        wait(ct.at[d, h], ct_r.at[d, h])
        if d in (7, 6) or (d == 5 and h == 0):
            ct_send(d, h, 1)
        if d in (1, 2) or (d == 3 and h == 1):
            ct_send(d, h, -1)

    def replica(d, e=0):
        return lax.rem(y + e, NY) * NZ + lax.rem(z + d, NZ)

    def gv_send(d, h, e):
        target = gv.at[replica(d), pl.ds(h * HALF, HALF)]
        send(gst.at[d, h, lax.rem(y + e, NY)], target, 4, gv_r.at[d], device(dy=e))

    def gradient(d, h):
        value = jnp.dot(ct[d, h], us[d].reshape(ROWS, SLICE), preferred_element_type=F32).astype(BF16)
        for j in range(NY):
            gst[d, h, j] = value[:, j * WIDE : (j + 1) * WIDE]
        for e in (2, 1, 3):
            gv_send(d, h, e)
        gv[replica(d), h * HALF : (h + 1) * HALF] = gst[d, h, y]

    def gram_pair(d1, d2):
        first = [replica(d1, e) for e in range(NY)]
        second = [replica(d2, e) for e in range(NY)]
        pairs = [(i, j) for i in range(NY) for j in range(NY) if d1 != d2 or i <= j]

        def body(step, sums):
            at = pl.ds(pl.multiple_of(step * 16, 16), 16)
            a = [gv[b, at].astype(F32) for b in first]
            bs = a if d1 == d2 else [gv[b, at].astype(F32) for b in second]
            return tuple(s + a[i] * bs[j] for s, (i, j) in zip(sums, pairs))

        sums = lax.fori_loop(0, HEADS // 16, body, tuple(jnp.zeros((16, WIDE), F32) for _ in pairs), unroll=16)
        for s, (i, j) in zip(sums, pairs):
            line = jnp.sum(s, axis=0, keepdims=True)
            zi, yi = lax.rem(z + d1, NZ), lax.rem(y + i, NY)
            zj, yj = lax.rem(z + d2, NZ), lax.rem(y + j, NY)
            acc[pl.ds(zi * 128 + yi * N_DP + yj * NZ + zj, 1), :] = line
            acc[pl.ds(zj * 128 + yj * N_DP + yi * NZ + zi, 1), :] = line

    done = []

    def gram(d):
        wait(gv.at[pl.ds(0, NY - 1)], gv_r.at[d])
        done.append(d)
        for other in done:
            gram_pair(d, other)

    us_own(0)
    for d in (1, 7, 2, 6, 3, 5, 4):
        aa_send(d)
    us_forward(0)
    for d in (1, 7):
        aa_ready(d)
        us_own(d)
    for h in range(2):
        ct_send(0, h, 1)
        ct_send(0, h, -1)
    us_share(0)
    for d in (2, 6):
        aa_ready(d)
        us_own(d)
    us_forward(1)
    us_forward(7)
    for d in (3, 5):
        aa_ready(d)
        us_own(d)
    us_share(1)
    us_share(7)
    us_forward(2)
    us_forward(6)
    aa_ready(4)
    us_own(4)
    us_share(2)
    us_share(6)
    us_ready(0)
    gradient(0, 0)
    gradient(0, 1)
    ct_arrived(7, 0)
    ct_arrived(1, 0)
    us_forward(3)
    us_forward(5)
    ct_arrived(7, 1)
    ct_arrived(1, 1)
    us_forward(4)
    us_share(3)
    us_share(5)
    for d in (1, 7):
        us_ready(d)
        gradient(d, 0)
        gradient(d, 1)
    us_share(4)
    uf_own(0)
    uf_own(1)
    us_ready(2)
    us_ready(6)
    for h in range(2):
        ct_arrived(6, h)
        ct_arrived(2, h)
        gradient(6, h)
        gradient(2, h)
    gram(0)
    gram(1)
    uf_forward()
    us_ready(3)
    us_ready(5)
    for h in range(2):
        ct_arrived(5, h)
        ct_arrived(3, h)
        gradient(5, h)
        gradient(3, h)
        if h == 0:
            gram(7)
    gram(2)
    gram(6)
    us_ready(4)
    for h in range(2):
        ct_arrived(4, h)
        gradient(4, h)
    uf_share()
    gram(3)
    gram(5)
    gram(4)

    ones = jnp.ones((8, 128), BF16)
    sums = acc[...]
    high = sums.astype(BF16)
    low = (sums - high.astype(F32)).astype(BF16)
    over_lanes = (((1,), (1,)), ((), ()))
    flat = lax.dot_general(ones, high, over_lanes, preferred_element_type=F32) + lax.dot_general(
        ones, low, over_lanes, preferred_element_type=F32
    )
    sub = lax.broadcasted_iota(jnp.int32, (8, 128), 0)
    tile = jnp.zeros((8, 128), F32)
    for i in range(8):
        tile = jnp.where(sub == i, flat[:, i * 128 : (i + 1) * 128], tile)
    src_a[...] = tile
    for k, (dz, dc) in enumerate(PEERS_A):
        send(src_a, in_a.at[k], 5, ab_r.at[0], device(dz=dz, dc=dc))

    load_w.wait()
    wait(uf.at[c], uf_r.at[3])
    over_width = (((1,), (1,)), ((), ()))
    parts = []
    for core in range(NC):
        rows = uf[core].reshape(NX * SHARD, D)
        parts.append(
            lax.dot_general(rows, wv[...], over_width, preferred_element_type=F32).astype(BF16)
        )
    gathered = jnp.concatenate(parts, axis=0)
    out_back[...] = lax.dot_general(pt[...], gathered, (((0,), (0,)), ((), ())), preferred_element_type=F32).astype(BF16)

    store_back = pltpu.make_async_copy(out_back, hbm_back, local.at[4])
    store_back.start()

    wait(in_a, ab_r.at[0])
    total = src_a[...]
    for k in range(len(PEERS_A)):
        total = total + in_a[k]
    src_b[...] = total
    for k, (dy, dx) in enumerate(PEERS_B):
        send(src_b, in_b.at[k], 6, ab_r.at[1], device(dy=dy, dx=dx))
    wait(in_b, ab_r.at[1])
    for k in range(len(PEERS_B)):
        total = total + in_b[k]

    quarter = [total] + [pltpu.roll(total, 128 - N_DP * q, 1) for q in range(1, NY)]
    m = jnp.concatenate(quarter, axis=0)
    row = lax.broadcasted_iota(jnp.int32, (N_DP, 128), 0)
    lane = lax.broadcasted_iota(jnp.int32, (N_DP, 128), 1)
    m = jnp.where(lane < N_DP, m, 0.0)
    weight = jnp.ones((N_DP, 1), F32)
    for level in range(5):
        bit = 1 << level
        own = jnp.where(lane == row, m, 0.0)
        mixed = jnp.where(lane == (row ^ bit), m, 0.0)
        down = 1.0 - jnp.sum(mixed, axis=1, keepdims=True) / (2.0 * (jnp.sum(own, axis=1, keepdims=True) + EPS))
        across = 1.0 - jnp.sum(mixed, axis=0, keepdims=True) / (2.0 * (jnp.sum(own, axis=0, keepdims=True) + EPS))
        weight = weight * down
        m = (down * across) * m
        m = m + jnp.where((row & bit) == 0, pltpu.roll(m, N_DP - bit, 0), pltpu.roll(m, bit, 0))
        m = m + jnp.where((lane & bit) == 0, pltpu.roll(m, 128 - bit, 1), pltpu.roll(m, bit, 1))
        m = jnp.where(lane < N_DP, m, 0.0)
    wts[...] = jnp.broadcast_to(weight, (N_DP, 128))

    def combine(step, _):
        at = pl.ds(pl.multiple_of(step * 16, 16), 16)
        value = jnp.zeros((16, WIDE), F32)
        for b in range(N_DP):
            value = value + gv[b, at].astype(F32) * wts[b : b + 1, :]
        out_grad[at, :] = value
        return 0

    lax.fori_loop(0, HEADS // 16, combine, 0, unroll=4)
    store_grad = pltpu.make_async_copy(out_grad, hbm_grad, local.at[5])
    store_grad.start()
    whole = (us.at[pl.ds(0, 7)], pack, us.at[pl.ds(0, 7)], ct.at[pl.ds(0, 7)], gv.at[pl.ds(0, 24)], in_a, in_b)
    for kind, ref in enumerate(whole):
        wait(ref, sent.at[kind])
    store_grad.wait()
    store_back.wait()


def hand_over(grad, back, out_grad, out_back):
    out_grad[...] = grad[...]
    out_back[...] = back[...]


def body(context, cotangent, row_order, out_weight):
    sem = pltpu.SemaphoreType.DMA
    grad, back = pl.pallas_call(
        kernel,
        out_shape=(
            jax.ShapeDtypeStruct((HEADS, WIDE), F32),
            jax.ShapeDtypeStruct((ROWS, HEADS), BF16),
        ),
        in_specs=[pl.BlockSpec(memory_space=pl.ANY)] * 4,
        out_specs=[pl.BlockSpec(memory_space=pltpu.HBM)] * 2,
        scratch_shapes=[
            pltpu.VMEM((HEADS, WIDE), F32),
            pltpu.VMEM((ROWS, HEADS), BF16),
            pltpu.VMEM((NC, NX, SHARD, D), BF16),
            pltpu.VMEM((NZ, NC, NX, SHARD, SLICE), BF16),
            pltpu.VMEM((NZ - 1, SHARD, SLICE), BF16),
            pltpu.VMEM((NZ, 2, HALF, ROWS), BF16),
            pltpu.VMEM((ROWS, HEADS), BF16),
            pltpu.VMEM((1, ROWS), jnp.int32),
            pltpu.VMEM((HEADS, D), BF16),
            pltpu.VMEM((ROWS, ROWS), BF16),
            pltpu.VMEM((NZ, 2, NY, HALF, WIDE), BF16),
            pltpu.VMEM((N_DP, HEADS, WIDE), BF16),
            pltpu.VMEM((N_DP * N_DP, 128), F32),
            pltpu.VMEM((8, 128), F32),
            pltpu.VMEM((8, 128), F32),
            pltpu.VMEM((len(PEERS_A), 8, 128), F32),
            pltpu.VMEM((len(PEERS_B), 8, 128), F32),
            pltpu.VMEM((N_DP, 128), F32),
            sem((6,)),
            sem((7,)),
            sem((NZ, 3)),
            sem((NZ,)),
            sem((4,)),
            sem((NZ, 2)),
            sem((NZ,)),
            sem((2,)),
        ],
        name="adasum",
        compiler_params=pltpu.CompilerParams(
            collective_id=0, has_side_effects=True, vmem_limit_bytes=63 << 20
        ),
        cost_estimate=pl.CostEstimate(flops=2_300_000_000, bytes_accessed=4_000_000, transcendentals=0),
    )(context, cotangent, row_order, out_weight)
    return pl.pallas_call(
        hand_over,
        out_shape=(jax.ShapeDtypeStruct(grad.shape, F32), jax.ShapeDtypeStruct(back.shape, BF16)),
        name="hand_over",
    )(grad, back)


def solution(mesh):
    in_specs = (P("dp", "tensor"), P(("dp", "tensor"), None), P("dp", None), P("tensor", None))
    out_specs = (P("tensor", "dp"), P("dp", "tensor"))
    return jax.shard_map(body, mesh=mesh, in_specs=in_specs, out_specs=out_specs, check_vma=False)
```

time: 82.1 us -> 70.4 us (0.86)
  Pallas kernels: 75.6 us -> 69.6 us
  local copies, waits for them, and re-layouts: 5.62 us -> 0 us
    pallas_call x1, Pallas kernels: 75.6 us -> 67.8 us  [body(): pl.pallas_call(kernel, out_shape=(jax.ShapeDtypeStruct((HEADS, WIDE), F32...]
    unnamed x10 -> x0, local copies, waits for them, and re-layouts: 5.62 us -> none
    pallas_call x0 -> x1, Pallas kernels: none -> 1.78 us  [body(): pl.pallas_call(hand_over, out_shape=(jax.ShapeDtypeStruct(grad.shape, F32...]
where the time goes in v2:
time: 70.4 us; the launch traced here: 70.2 us
  Pallas kernels  69.6 us (99%)
    pallas_call x1, Pallas kernels, body(): pl.pallas_call(kernel, out_shape=(jax.ShapeDtypeStruct((HEADS, WIDE), F32...  67.8 us
    pallas_call x1, Pallas kernels, body(): pl.pallas_call(hand_over, out_shape=(jax.ShapeDtypeStruct(grad.shape, F32...  1.78 us

profile of v2, /device:TPU:1, one launch (start us, length us, event | category | flops | bytes accessed | tf_op | source)
XLA Modules:
  0.0 70.2 jit_solution(220289388263503436)
XLA Ops:
  0.6 67.8 %adasum.1 = (f32[256,128]{1,0:T(8,128)}, bf16[512,256]{1,0:T(8,128)(2,1)}) custom-call(bf16[512,256]{1,0:T(8,128)(2,1)} %context.1, bf16[64,4096]{1,0:T(8,128)(2,1)} %cotangent.1, s32[1,512]{1,0:T(1,128)} %row_order.1, bf16[256,4096]{1,0:T(8,128)(2,1)} %out_weight.1), custom_call_target="tpu_custom_call" | custom-call | flops 2300000000 | bytes 4000000 | tf_op jit(solution)/shard_map/adasum/pallas_call | solution.py:350
  68.5 1.8 %hand_over.1 = (f32[256,128]{1,0:T(8,128)}, bf16[512,256]{1,0:T(8,128)(2,1)}) custom-call(f32[256,128]{1,0:T(8,128)} %get-tuple-element.4.grad, bf16[512,256]{1,0:T(8,128)(2,1)} %get-tuple-element.5.back), custom_call_target="tpu_custom_call" | custom-call | tf_op jit(solution)/shard_map/hand_over/pallas_call | solution.py:392

commit v3 on v2

--- a/solution.py
+++ b/solution.py
@@ -21,7 +21,7 @@
 
 
 def kernel(
-    context, cotangent, row_order, out_weight, hbm_grad, hbm_back, out_grad, out_back,
+    context, cotangent, row_order, out_weight, out_grad, out_back,
     uf, us, pack, ct, cv, ov, wv, pt, gst, gv, acc, src_a, src_b, in_a, in_b, wts,
     local, sent, us_r, aa_r, uf_r, ct_r, gv_r, ab_r,
 ):
@@ -78,29 +78,22 @@
     ct[0, 1] = mine[HALF:]
     pl.semaphore_wait(barrier, len(NEIGHBOURS))
 
-    right, left, sibling = device(dx=1), device(dx=NX - 1), device(dc=1)
+    right, left, far, sibling = device(dx=1), device(dx=NX - 1), device(dx=2), device(dc=1)
     xl, xr, xf = lax.rem(x + NX - 1, NX), lax.rem(x + 1, NX), lax.rem(x + 2, NX)
     lo, hi = pl.ds(0, SHARD // 2), pl.ds(SHARD // 2, SHARD // 2)
 
     def us_own(d):
         mine = us.at[d, c, x]
-        send(mine, mine, 0, us_r.at[d, 0], right)
-        send(mine, mine, 0, us_r.at[d, 0], left)
-
-    def us_forward(d):
-        wait(us.at[d, c, pl.ds(0, 2)], us_r.at[d, 0])
-        part = us.at[d, c, xl, lo]
-        send(part, part, 0, us_r.at[d, 1], right)
-        part = us.at[d, c, xr, hi]
-        send(part, part, 0, us_r.at[d, 1], left)
+        for to in (far, right, left):
+            send(mine, mine, 0, us_r.at[d, 0], to)
 
     def us_share(d):
-        wait(us.at[d, c, 0], us_r.at[d, 1])
+        wait(us.at[d, c, pl.ds(0, 3)], us_r.at[d, 0])
         part = us.at[d, c]
-        send(part, part, 0, us_r.at[d, 2], sibling)
+        send(part, part, 0, us_r.at[d, 1], sibling)
 
     def us_ready(d):
-        wait(us.at[d, c], us_r.at[d, 2])
+        wait(us.at[d, c], us_r.at[d, 1])
 
     def aa_send(d):
         send(pack.at[d - 1], us.at[NZ - d, c, x], 1, aa_r.at[NZ - d], device(dz=d))
@@ -123,11 +116,13 @@
         part = uf.at[c, xr, hi]
         send(part, part, 2, uf_r.at[2], left)
 
-    def uf_share():
+    def uf_share_near():
         wait(uf.at[c, x], uf_r.at[1])
         for at in (xl, xr):
             part = uf.at[c, at]
             send(part, part, 2, uf_r.at[3], sibling)
+
+    def uf_share_far():
         wait(uf.at[c, x], uf_r.at[2])
         part = uf.at[c, xf]
         send(part, part, 2, uf_r.at[3], sibling)
@@ -186,77 +181,76 @@
             gram_pair(d, other)
 
     us_own(0)
-    for d in (1, 7, 2, 6, 3, 5, 4):
+    for d in (1, 7, 2, 6):
         aa_send(d)
-    us_forward(0)
+    for h in range(2):
+        ct_send(0, h, 1)
+        ct_send(0, 1 - h, -1)
     for d in (1, 7):
         aa_ready(d)
         us_own(d)
-    for h in range(2):
-        ct_send(0, h, 1)
-        ct_send(0, h, -1)
     us_share(0)
     for d in (2, 6):
         aa_ready(d)
         us_own(d)
-    us_forward(1)
-    us_forward(7)
+    for d in (3, 5, 4):
+        aa_send(d)
+    us_share(1)
+    us_share(7)
+    us_ready(0)
+    gradient(0, 0)
+    gradient(0, 1)
+    us_share(2)
+    us_share(6)
+    for h in range(2):
+        ct_arrived(7, h)
+        ct_arrived(1, 1 - h)
+    us_ready(1)
+    us_ready(7)
+    for h in range(2):
+        gradient(7, h)
+        gradient(1, 1 - h)
     for d in (3, 5):
         aa_ready(d)
         us_own(d)
-    us_share(1)
-    us_share(7)
-    us_forward(2)
-    us_forward(6)
     aa_ready(4)
     us_own(4)
-    us_share(2)
-    us_share(6)
-    us_ready(0)
-    gradient(0, 0)
-    gradient(0, 1)
-    ct_arrived(7, 0)
-    ct_arrived(1, 0)
-    us_forward(3)
-    us_forward(5)
-    ct_arrived(7, 1)
-    ct_arrived(1, 1)
-    us_forward(4)
+    us_ready(2)
+    us_ready(6)
+    ct_arrived(6, 0)
+    ct_arrived(2, 1)
+    gradient(6, 0)
+    gradient(2, 1)
+    ct_arrived(6, 1)
+    ct_arrived(2, 0)
+    gradient(6, 1)
+    gradient(2, 0)
     us_share(3)
     us_share(5)
-    for d in (1, 7):
-        us_ready(d)
-        gradient(d, 0)
-        gradient(d, 1)
+    gram(0)
+    gram(1)
     us_share(4)
     uf_own(0)
     uf_own(1)
-    us_ready(2)
-    us_ready(6)
-    for h in range(2):
-        ct_arrived(6, h)
-        ct_arrived(2, h)
-        gradient(6, h)
-        gradient(2, h)
-    gram(0)
-    gram(1)
-    uf_forward()
     us_ready(3)
     us_ready(5)
-    for h in range(2):
-        ct_arrived(5, h)
-        ct_arrived(3, h)
-        gradient(5, h)
-        gradient(3, h)
-        if h == 0:
-            gram(7)
+    ct_arrived(5, 0)
+    ct_arrived(3, 1)
+    gradient(5, 0)
+    gradient(3, 1)
+    gram(7)
+    ct_arrived(5, 1)
+    ct_arrived(3, 0)
+    gradient(5, 1)
+    gradient(3, 0)
+    us_ready(4)
     gram(2)
     gram(6)
-    us_ready(4)
-    for h in range(2):
-        ct_arrived(4, h)
-        gradient(4, h)
-    uf_share()
+    ct_arrived(4, 0)
+    gradient(4, 0)
+    ct_arrived(4, 1)
+    gradient(4, 1)
+    uf_forward()
     gram(3)
     gram(5)
     gram(4)
@@ -277,6 +271,15 @@
     for k, (dz, dc) in enumerate(PEERS_A):
         send(src_a, in_a.at[k], 5, ab_r.at[0], device(dz=dz, dc=dc))
 
+    uf_share_near()
+    wait(in_a, ab_r.at[0])
+    total = src_a[...]
+    for k in range(len(PEERS_A)):
+        total = total + in_a[k]
+    src_b[...] = total
+    for k, (dy, dx) in enumerate(PEERS_B):
+        send(src_b, in_b.at[k], 6, ab_r.at[1], device(dy=dy, dx=dx))
+    uf_share_far()
     load_w.wait()
     wait(uf.at[c], uf_r.at[3])
     over_width = (((1,), (1,)), ((), ()))
@@ -289,16 +292,6 @@
     gathered = jnp.concatenate(parts, axis=0)
     out_back[...] = lax.dot_general(pt[...], gathered, (((0,), (0,)), ((), ())), preferred_element_type=F32).astype(BF16)
 
-    store_back = pltpu.make_async_copy(out_back, hbm_back, local.at[4])
-    store_back.start()
-
-    wait(in_a, ab_r.at[0])
-    total = src_a[...]
-    for k in range(len(PEERS_A)):
-        total = total + in_a[k]
-    src_b[...] = total
-    for k, (dy, dx) in enumerate(PEERS_B):
-        send(src_b, in_b.at[k], 6, ab_r.at[1], device(dy=dy, dx=dx))
     wait(in_b, ab_r.at[1])
     for k in range(len(PEERS_B)):
         total = total + in_b[k]
@@ -331,18 +324,9 @@
         return 0
 
     lax.fori_loop(0, HEADS // 16, combine, 0, unroll=4)
-    store_grad = pltpu.make_async_copy(out_grad, hbm_grad, local.at[5])
-    store_grad.start()
     whole = (us.at[pl.ds(0, 7)], pack, us.at[pl.ds(0, 7)], ct.at[pl.ds(0, 7)], gv.at[pl.ds(0, 24)], in_a, in_b)
     for kind, ref in enumerate(whole):
         wait(ref, sent.at[kind])
-    store_grad.wait()
-    store_back.wait()
-
-
-def hand_over(grad, back, out_grad, out_back):
-    out_grad[...] = grad[...]
-    out_back[...] = back[...]
 
 
 def body(context, cotangent, row_order, out_weight):
@@ -354,10 +338,8 @@
             jax.ShapeDtypeStruct((ROWS, HEADS), BF16),
         ),
         in_specs=[pl.BlockSpec(memory_space=pl.ANY)] * 4,
-        out_specs=[pl.BlockSpec(memory_space=pltpu.HBM)] * 2,
+        out_specs=[pl.BlockSpec(memory_space=pltpu.VMEM)] * 2,
         scratch_shapes=[
-            pltpu.VMEM((HEADS, WIDE), F32),
-            pltpu.VMEM((ROWS, HEADS), BF16),
             pltpu.VMEM((NC, NX, SHARD, D), BF16),
             pltpu.VMEM((NZ, NC, NX, SHARD, SLICE), BF16),
             pltpu.VMEM((NZ - 1, SHARD, SLICE), BF16),
@@ -374,9 +356,9 @@
             pltpu.VMEM((len(PEERS_A), 8, 128), F32),
             pltpu.VMEM((len(PEERS_B), 8, 128), F32),
             pltpu.VMEM((N_DP, 128), F32),
-            sem((6,)),
+            sem((4,)),
             sem((7,)),
-            sem((NZ, 3)),
+            sem((NZ, 2)),
             sem((NZ,)),
             sem((4,)),
             sem((NZ, 2)),
@@ -385,15 +367,11 @@
         ],
         name="adasum",
         compiler_params=pltpu.CompilerParams(
-            collective_id=0, has_side_effects=True, vmem_limit_bytes=63 << 20
+            collective_id=0, has_side_effects=True, vmem_limit_bytes=int(53.5 * 2**20)
         ),
         cost_estimate=pl.CostEstimate(flops=2_300_000_000, bytes_accessed=4_000_000, transcendentals=0),
     )(context, cotangent, row_order, out_weight)
-    return pl.pallas_call(
-        hand_over,
-        out_shape=(jax.ShapeDtypeStruct(grad.shape, F32), jax.ShapeDtypeStruct(back.shape, BF16)),
-        name="hand_over",
-    )(grad, back)
+    return grad, back
 
 
 def solution(mesh):

time: 70.4 us -> 64.1 us (0.911)
  Pallas kernels: 69.6 us -> 61.3 us
  local copies, waits for them, and re-layouts: 0 us -> 2.03 us
    pallas_call x1, Pallas kernels: 67.8 us -> 61.3 us  [body(): pl.pallas_call(kernel, out_shape=(jax.ShapeDtypeStruct((HEADS, WIDE), F32...]
    unnamed x0 -> x4, local copies, waits for them, and re-layouts: none -> 2.03 us
    pallas_call x1 -> x0, Pallas kernels: 1.78 us -> none  [body(): pl.pallas_call(hand_over, out_shape=(jax.ShapeDtypeStruct(grad.shape, F32...]
where the time goes in v3:
time: 64.1 us; the launch traced here: 63.9 us
  Pallas kernels  61.3 us (96%)
  local copies, waits for them, and re-layouts  2.03 us (3%)
  between operations  0.65 us (1%)
    pallas_call x1, Pallas kernels, body(): pl.pallas_call(kernel, out_shape=(jax.ShapeDtypeStruct((HEADS, WIDE), F32...  61.3 us
    unnamed x4, local copies, waits for them, and re-layouts  2.03 us

profile of v3, /device:TPU:1, one launch (start us, length us, event | category | flops | bytes accessed | tf_op | source)
XLA Modules:
  0.0 63.9 jit_solution(17726560672845961366)
XLA Ops:
  0.6 0.0 copy-start
  0.6 0.7 %copy-done = s32[1,512]{1,0:T(1,128)S(1)} copy-done((s32[1,512]{1,0:T(1,128)S(1)}, s32[1,512]{1,0:T(1,128)}, u32[]{:S(2)}) %copy-start) | copy-done | bytes 2072
  1.3 61.3 %adasum.1 = (f32[256,128]{1,0:T(8,128)S(1)}, bf16[512,256]{1,0:T(8,128)(2,1)S(1)}) custom-call(bf16[512,256]{1,0:T(8,128)(2,1)} %context.1, bf16[64,4096]{1,0:T(8,128)(2,1)} %cotangent.1, s32[1,512]{1,0:T(1,128)S(1)} %copy-done, bf16[256,4096]{1,0:T(8,128)(2,1)} %out_weight.1), custom_call_target="tpu_custom_call" | custom-call | flops 2300000000 | bytes 4000000 | tf_op jit(solution)/shard_map/adasum/pallas_call | solution.py:334
  62.6 0.7 %copy.8 = f32[256,128]{1,0:T(8,128)} copy(f32[256,128]{1,0:T(8,128)S(1)} %get-tuple-element.4) | data formatting | bytes 262144
  63.2 0.7 %copy.9 = bf16[512,256]{1,0:T(8,128)(2,1)} copy(bf16[512,256]{1,0:T(8,128)(2,1)S(1)} %get-tuple-element.5) | data formatting | bytes 524288
Async XLA Ops:
  0.6 0.7 %copy-start = (s32[1,512]{1,0:T(1,128)S(1)}, s32[1,512]{1,0:T(1,128)}, u32[]{:S(2)}) copy-start(s32[1,512]{1,0:T(1,128)} %row_order.1) | copy-start | bytes 6148

commit v4 on v3

--- a/solution.py
+++ b/solution.py
@@ -17,7 +17,7 @@
 N_DP = NY * NZ
 PEERS_A = [(dz, dc) for dz in (4, 3, 5, 2, 6, 1, 7, 0) for dc in (1, 0) if dz or dc]
 PEERS_B = [(dy, dx) for dy, dx in sorted(((a, b) for a in range(NY) for b in range(NX)), key=lambda p: -min(p[0], NY - p[0]) - min(p[1], NX - p[1])) if dy or dx]
-NEIGHBOURS = [(0, dz, 0, 0) for dz in (4, 3, 5, 2, 6, 1, 7)] + [(dy, 0, 0, 0) for dy in (2, 1, 3)] + [(0, 0, dx, 0) for dx in (2, 1, 3)] + [(0, 0, 0, 1)]
+NEIGHBOURS = [(0, dz, 0, 0) for dz in (2, 6, 1, 7)] + [(dy, 0, 0, 0) for dy in (2, 1, 3)] + [(0, 0, dx, 0) for dx in (2, 1, 3)] + [(0, 0, 0, 1)]
 
 
 def kernel(
@@ -143,7 +143,7 @@
 
     def gv_send(d, h, e):
         target = gv.at[replica(d), pl.ds(h * HALF, HALF)]
-        send(gst.at[d, h, lax.rem(y + e, NY)], target, 4, gv_r.at[d], device(dy=e))
+        send(gst.at[d, h, lax.rem(y + e, NY)], target, 4, gv_r.at[d, h], device(dy=e))
 
     def gradient(d, h):
         value = jnp.dot(ct[d, h], us[d].reshape(ROWS, SLICE), preferred_element_type=F32).astype(BF16)
@@ -153,32 +153,36 @@
             gv_send(d, h, e)
         gv[replica(d), h * HALF : (h + 1) * HALF] = gst[d, h, y]
 
-    def gram_pair(d1, d2):
+    def gram_pair(d1, d2, h):
         first = [replica(d1, e) for e in range(NY)]
         second = [replica(d2, e) for e in range(NY)]
         pairs = [(i, j) for i in range(NY) for j in range(NY) if d1 != d2 or i <= j]
 
         def body(step, sums):
-            at = pl.ds(pl.multiple_of(step * 16, 16), 16)
+            at = pl.ds(pl.multiple_of(h * HALF + step * 16, 16), 16)
             a = [gv[b, at].astype(F32) for b in first]
             bs = a if d1 == d2 else [gv[b, at].astype(F32) for b in second]
             return tuple(s + a[i] * bs[j] for s, (i, j) in zip(sums, pairs))
 
-        sums = lax.fori_loop(0, HEADS // 16, body, tuple(jnp.zeros((16, WIDE), F32) for _ in pairs), unroll=16)
+        sums = lax.fori_loop(0, HALF // 16, body, tuple(jnp.zeros((16, WIDE), F32) for _ in pairs), unroll=8)
         for s, (i, j) in zip(sums, pairs):
             line = jnp.sum(s, axis=0, keepdims=True)
             zi, yi = lax.rem(z + d1, NZ), lax.rem(y + i, NY)
             zj, yj = lax.rem(z + d2, NZ), lax.rem(y + j, NY)
-            acc[pl.ds(zi * 128 + yi * N_DP + yj * NZ + zj, 1), :] = line
-            acc[pl.ds(zj * 128 + yj * N_DP + yi * NZ + zi, 1), :] = line
-
-    done = []
+            acc[h, pl.ds(zi * 128 + yi * N_DP + yj * NZ + zj, 1), :] = line
+            acc[h, pl.ds(zj * 128 + yj * N_DP + yi * NZ + zi, 1), :] = line
+
+    done = ([], [])
+
+    def gram_half(d, h):
+        wait(gv.at[pl.ds(0, NY - 1), pl.ds(0, HALF)], gv_r.at[d, h])
+        done[h].append(d)
+        for other in done[h]:
+            gram_pair(d, other, h)
 
     def gram(d):
-        wait(gv.at[pl.ds(0, NY - 1)], gv_r.at[d])
-        done.append(d)
-        for other in done:
-            gram_pair(d, other)
+        for h in range(2):
+            gram_half(d, h)
 
     us_own(0)
     for d in (1, 7, 2, 6):
@@ -221,12 +225,12 @@
     ct_arrived(2, 1)
     gradient(6, 0)
     gradient(2, 1)
+    us_share(3)
+    us_share(5)
     ct_arrived(6, 1)
     ct_arrived(2, 0)
     gradient(6, 1)
     gradient(2, 0)
-    us_share(3)
-    us_share(5)
     gram(0)
     gram(1)
     us_share(4)
@@ -251,12 +255,15 @@
     ct_arrived(4, 1)
     gradient(4, 1)
     uf_forward()
-    gram(3)
-    gram(5)
-    gram(4)
+    gram_half(5, 0)
+    gram_half(3, 1)
+    gram_half(5, 1)
+    gram_half(3, 0)
+    gram_half(4, 0)
+    gram_half(4, 1)
 
     ones = jnp.ones((8, 128), BF16)
-    sums = acc[...]
+    sums = acc[0] + acc[1]
     high = sums.astype(BF16)
     low = (sums - high.astype(F32)).astype(BF16)
     over_lanes = (((1,), (1,)), ((), ()))
@@ -331,7 +338,7 @@
 
 def body(context, cotangent, row_order, out_weight):
     sem = pltpu.SemaphoreType.DMA
-    grad, back = pl.pallas_call(
+    return pl.pallas_call(
         kernel,
         out_shape=(
             jax.ShapeDtypeStruct((HEADS, WIDE), F32),
@@ -350,7 +357,7 @@
             pltpu.VMEM((ROWS, ROWS), BF16),
             pltpu.VMEM((NZ, 2, NY, HALF, WIDE), BF16),
             pltpu.VMEM((N_DP, HEADS, WIDE), BF16),
-            pltpu.VMEM((N_DP * N_DP, 128), F32),
+            pltpu.VMEM((2, N_DP * N_DP, 128), F32),
             pltpu.VMEM((8, 128), F32),
             pltpu.VMEM((8, 128), F32),
             pltpu.VMEM((len(PEERS_A), 8, 128), F32),
@@ -362,7 +369,7 @@
             sem((NZ,)),
             sem((4,)),
             sem((NZ, 2)),
-            sem((NZ,)),
+            sem((NZ, 2)),
             sem((2,)),
         ],
         name="adasum",
@@ -371,7 +378,6 @@
         ),
         cost_estimate=pl.CostEstimate(flops=2_300_000_000, bytes_accessed=4_000_000, transcendentals=0),
     )(context, cotangent, row_order, out_weight)
-    return grad, back
 
 
 def solution(mesh):

time: 64.1 us -> 62.3 us (0.972)
  Pallas kernels: 61.3 us -> 59.5 us
    pallas_call x1, Pallas kernels: 61.3 us -> 59.5 us  [body(): pl.pallas_call(kernel, out_shape=(jax.ShapeDtypeStruct((HEADS, WIDE), F32...]
where the time goes in v4:
time: 62.3 us; the launch traced here: 62.2 us
  Pallas kernels  59.5 us (96%)
  local copies, waits for them, and re-layouts  2.03 us (3%)
  between operations  0.65 us (1%)
    pallas_call x1, Pallas kernels, body(): pl.pallas_call(kernel, out_shape=(jax.ShapeDtypeStruct((HEADS, WIDE), F32...  59.5 us
    unnamed x4, local copies, waits for them, and re-layouts  2.03 us

profile of v4, /device:TPU:1, one launch (start us, length us, event | category | flops | bytes accessed | tf_op | source)
XLA Modules:
  0.0 62.2 jit_solution(4582632526702711203)
XLA Ops:
  0.6 0.0 copy-start
  0.6 0.7 %copy-done = s32[1,512]{1,0:T(1,128)S(1)} copy-done((s32[1,512]{1,0:T(1,128)S(1)}, s32[1,512]{1,0:T(1,128)}, u32[]{:S(2)}) %copy-start) | copy-done | bytes 2072
  1.3 59.5 %adasum.1 = (f32[256,128]{1,0:T(8,128)S(1)}, bf16[512,256]{1,0:T(8,128)(2,1)S(1)}) custom-call(bf16[512,256]{1,0:T(8,128)(2,1)} %context.1, bf16[64,4096]{1,0:T(8,128)(2,1)} %cotangent.1, s32[1,512]{1,0:T(1,128)S(1)} %copy-done, bf16[256,4096]{1,0:T(8,128)(2,1)} %out_weight.1), custom_call_target="tpu_custom_call" | custom-call | flops 2300000000 | bytes 4000000 | tf_op jit(solution)/shard_map/adasum/pallas_call | solution.py:341
  60.8 0.7 %copy.8 = f32[256,128]{1,0:T(8,128)} copy(f32[256,128]{1,0:T(8,128)S(1)} %get-tuple-element.4) | data formatting | bytes 262144
  61.5 0.7 %copy.9 = bf16[512,256]{1,0:T(8,128)(2,1)} copy(bf16[512,256]{1,0:T(8,128)(2,1)S(1)} %get-tuple-element.5) | data formatting | bytes 524288
Async XLA Ops:
  0.6 0.7 %copy-start = (s32[1,512]{1,0:T(1,128)S(1)}, s32[1,512]{1,0:T(1,128)}, u32[]{:S(2)}) copy-start(s32[1,512]{1,0:T(1,128)} %row_order.1) | copy-start | bytes 6148

commit v5 on v4

--- a/solution.py
+++ b/solution.py
@@ -48,16 +48,18 @@
     for step in NEIGHBOURS:
         pl.semaphore_signal(barrier, inc=1, device_id=device(*step), device_id_type=MESH)
 
-    load_cot = pltpu.make_async_copy(cotangent, uf.at[c, x], local.at[0])
+    quarters = [pl.ds(q * SHARD // 4, SHARD // 4) for q in range(4)]
+    load_cot = [pltpu.make_async_copy(cotangent.at[q], uf.at[c, x, q], local.at[4 + k]) for k, q in enumerate(quarters)]
     load_ctx = pltpu.make_async_copy(context, cv, local.at[1])
     load_ord = pltpu.make_async_copy(row_order, ov, local.at[2])
     load_w = pltpu.make_async_copy(out_weight, wv, local.at[3])
-    load_cot.start()
+    for copy in load_cot:
+        copy.start()
     load_ctx.start()
     load_ord.start()
-    load_w.start()
-
-    load_cot.wait()
+
+    for copy in load_cot:
+        copy.wait()
     for d in range(NZ):
         to = lax.rem(z + d, NZ)
         for j in range(NY):
@@ -184,6 +186,7 @@
         for h in range(2):
             gram_half(d, h)
 
+    load_w.start()
     us_own(0)
     for d in (1, 7, 2, 6):
         aa_send(d)
@@ -307,7 +310,6 @@
     m = jnp.concatenate(quarter, axis=0)
     row = lax.broadcasted_iota(jnp.int32, (N_DP, 128), 0)
     lane = lax.broadcasted_iota(jnp.int32, (N_DP, 128), 1)
-    m = jnp.where(lane < N_DP, m, 0.0)
     weight = jnp.ones((N_DP, 1), F32)
     for level in range(5):
         bit = 1 << level
@@ -319,7 +321,6 @@
         m = (down * across) * m
         m = m + jnp.where((row & bit) == 0, pltpu.roll(m, N_DP - bit, 0), pltpu.roll(m, bit, 0))
         m = m + jnp.where((lane & bit) == 0, pltpu.roll(m, 128 - bit, 1), pltpu.roll(m, bit, 1))
-        m = jnp.where(lane < N_DP, m, 0.0)
     wts[...] = jnp.broadcast_to(weight, (N_DP, 128))
 
     def combine(step, _):
@@ -330,7 +331,7 @@
         out_grad[at, :] = value
         return 0
 
-    lax.fori_loop(0, HEADS // 16, combine, 0, unroll=4)
+    lax.fori_loop(0, HEADS // 16, combine, 0, unroll=16)
     whole = (us.at[pl.ds(0, 7)], pack, us.at[pl.ds(0, 7)], ct.at[pl.ds(0, 7)], gv.at[pl.ds(0, 24)], in_a, in_b)
     for kind, ref in enumerate(whole):
         wait(ref, sent.at[kind])
@@ -363,7 +364,7 @@
             pltpu.VMEM((len(PEERS_A), 8, 128), F32),
             pltpu.VMEM((len(PEERS_B), 8, 128), F32),
             pltpu.VMEM((N_DP, 128), F32),
-            sem((4,)),
+            sem((8,)),
             sem((7,)),
             sem((NZ, 2)),
             sem((NZ,)),

time: 62.3 us -> 62.3 us (level)
  no operation moved by 1% of the time
where the time goes in v5:
time: 62.3 us; the launch traced here: 62.2 us
  Pallas kernels  59.5 us (96%)
  local copies, waits for them, and re-layouts  2.03 us (3%)
  between operations  0.65 us (1%)
    pallas_call x1, Pallas kernels, body(): pl.pallas_call(kernel, out_shape=(jax.ShapeDtypeStruct((HEADS, WIDE), F32...  59.5 us
    unnamed x4, local copies, waits for them, and re-layouts  2.03 us

profile of v5, /device:TPU:1, one launch (start us, length us, event | category | flops | bytes accessed | tf_op | source)
XLA Modules:
  0.0 62.2 jit_solution(15148257952125561410)
XLA Ops:
  0.6 0.0 copy-start
  0.6 0.7 %copy-done = s32[1,512]{1,0:T(1,128)S(1)} copy-done((s32[1,512]{1,0:T(1,128)S(1)}, s32[1,512]{1,0:T(1,128)}, u32[]{:S(2)}) %copy-start) | copy-done | bytes 2072
  1.3 59.5 %adasum.1 = (f32[256,128]{1,0:T(8,128)S(1)}, bf16[512,256]{1,0:T(8,128)(2,1)S(1)}) custom-call(bf16[512,256]{1,0:T(8,128)(2,1)} %context.1, bf16[64,4096]{1,0:T(8,128)(2,1)} %cotangent.1, s32[1,512]{1,0:T(1,128)S(1)} %copy-done, bf16[256,4096]{1,0:T(8,128)(2,1)} %out_weight.1), custom_call_target="tpu_custom_call" | custom-call | flops 2300000000 | bytes 4000000 | tf_op jit(solution)/shard_map/adasum/pallas_call | solution.py:342
  60.8 0.7 %copy.8 = f32[256,128]{1,0:T(8,128)} copy(f32[256,128]{1,0:T(8,128)S(1)} %get-tuple-element.4) | data formatting | bytes 262144
  61.5 0.7 %copy.9 = bf16[512,256]{1,0:T(8,128)(2,1)} copy(bf16[512,256]{1,0:T(8,128)(2,1)S(1)} %get-tuple-element.5) | data formatting | bytes 524288
Async XLA Ops:
  0.6 0.7 %copy-start = (s32[1,512]{1,0:T(1,128)S(1)}, s32[1,512]{1,0:T(1,128)}, u32[]{:S(2)}) copy-start(s32[1,512]{1,0:T(1,128)} %row_order.1) | copy-start | bytes 6148
